TPU v7x, 512 devices: a whole 4x4x16 slice. The times are simulated.
512 devices in a mesh: pipe: 2 (over core), dp: 16 (over y, x), tensor: 16 (over z).
Axes of the slice: x: 4, y: 4, z: 16, core: 2. Of those that a mesh axis runs over, the one named last changes fastest.
Arguments:
- x_act: bfloat16 [2, 6144, 16384], P('pipe', 'dp', 'tensor'), may hold values from -6 to 6
- grad_z: bfloat16 [2, 6144, 26624], P('pipe', 'dp', 'tensor'), may hold values from -6 to 6
- weight_tiles: bfloat16 [2, 256, 128, 128], P('pipe', 'tensor'), may hold values from -0.5 to 0.5
- tile_rows: int32 [2, 256], P('pipe', 'tensor'), may hold values from 0 to 127, as said below
- tile_cols: int32 [2, 256], P('pipe', 'tensor'), may hold values from 0 to 12
- err_in: float32 [2, 16, 256, 128, 128], P('pipe', 'dp', 'tensor'), may hold values from -0.3 to 0.3
- kept_mask: int32 [2, 16, 256], P('pipe', 'dp', 'tensor'), may hold values 0 or 1
- tile_list: int32 [2, 16, 192], P('pipe', 'dp', 'tensor'), may hold values from 0 to 23, as said below
- live_count: int32 [2, 16, 16], P('pipe', 'dp', 'tensor'), may hold values from 1 to 12, as said below
Outputs:
- recv_tiles: bfloat16 [2, 16, 192, 128, 128], P('pipe', 'dp', 'tensor')
- err_out: float32 [2, 16, 256, 128, 128], P('pipe', 'dp', 'tensor')
- grad_sum: float32 [2, 16, 16, 128, 128], P('pipe', 'dp', 'tensor')
Inputs may be any that keep to these rules, and one draw needn't show every extreme that they name: `tile_rows`: entry j of a tensor rank's 16 entries of one section names a column block held by tensor rank j // (16 / 16), that is one of the blocks ((j // (16 / 16)) * L to that plus L - 1, L = 16384 / (128 * 16)). `tile_list`: A device's 12 entries are distinct tile numbers m * L + b of its own region (L = 16384 / (128 * 16), m < 3, b < L). `live_count`: some device uses all 12 entries of its list.
All inputs are finite; a program needn't handle non-finite values. No bound on the sum of `kept_mask` on one device may be relied on, other than what follows from the above.
Results may differ from a plain program's by a relative error of at most 0.0048.
Values may be sent and summed in bfloat16 or wider, within the bound.
A program may use at most 128 MiB of HBM per device.

v0:
```python
import jax
import jax.numpy as jnp
from jax import lax
from jax.sharding import PartitionSpec as P


def shifted(value, axis, by):
    count = lax.axis_size(axis)
    return lax.ppermute(value, axis, [(i, (i + by) % count) for i in range(count)])


def pack_listed(input_grad, listed, live_now, tile_size, local_blocks):
    tok_count = input_grad.shape[0]
    grid = input_grad.reshape(tok_count // tile_size, tile_size, local_blocks, tile_size)
    picked = grid[listed // local_blocks, :, listed % local_blocks, :]
    valid = jnp.arange(listed.shape[0], dtype=jnp.int32) < live_now[0]
    return jnp.where(valid[:, None, None], picked, jnp.zeros_like(picked))


def local(
    x_act, grad_z, weight_tiles, tile_rows, tile_cols, err_in, kept_mask, tile_list, live_count
):
    tensor_count = lax.axis_size("tensor")
    inputs = x_act[0]
    grads_out = grad_z[0]
    stored = weight_tiles[0]
    row_ids = tile_rows[0]
    col_ids = tile_cols[0]
    tok_count = inputs.shape[0]
    tile_size = stored.shape[1]
    local_blocks = inputs.shape[1] // tile_size
    local_rows = row_ids % local_blocks
    grad_blocks = grads_out.reshape(tok_count, grads_out.shape[1] // tile_size, tile_size)
    grad_sel = jnp.take(grad_blocks, col_ids, axis=1)
    gathered = lax.all_gather(inputs, "tensor", axis=1, tiled=True)
    input_sel = jnp.take(
        gathered.reshape(tok_count, local_blocks * tensor_count, tile_size), row_ids, axis=1
    )
    weight_grads = jnp.einsum(
        "tkc,tkf->kcf", input_sel, grad_sel, preferred_element_type=jnp.float32
    ) * (1.0 / tok_count)
    accumulated = weight_grads + err_in[0, 0]
    keep_now = (kept_mask[0, 0] == 1)[:, None, None]
    sent_tiles = jnp.where(keep_now, accumulated, jnp.float32(0.0))
    residual = accumulated - sent_tiles
    summed = lax.psum_scatter(sent_tiles, "dp", scatter_dimension=0, tiled=True)
    partial_value = jnp.einsum(
        "tkf,kcf->tkc", grad_sel, stored, preferred_element_type=jnp.float32
    ).astype(jnp.bfloat16)
    arrived_terms, arrived_rows = (
        lax.all_to_all(partial_value, "tensor", split_axis=1, concat_axis=1, tiled=True),
        lax.all_to_all(local_rows[None, :], "tensor", split_axis=1, concat_axis=1, tiled=True),
    )
    onehot = (
        arrived_rows[0][:, None] == jnp.arange(local_blocks, dtype=jnp.int32)[None, :]
    ).astype(jnp.bfloat16)
    input_grad = jnp.einsum(
        "trc,rb->tbc", arrived_terms, onehot, preferred_element_type=jnp.float32
    ).astype(jnp.bfloat16)
    listed = tile_list[0, 0]
    live_now = live_count[0, 0]
    grad_in, listed_in, live_in = shifted((input_grad, listed, live_now), "pipe", -1)
    arrived = pack_listed(grad_in, listed_in, live_in, tile_size, local_blocks)
    return (arrived[None, None], residual[None, None], summed[None, None])


def solution(mesh):
    return jax.shard_map(
        local,
        mesh=mesh,
        in_specs=(
            P("pipe", "dp", "tensor"),
            P("pipe", "dp", "tensor"),
            P("pipe", "tensor", None, None),
            P("pipe", "tensor"),
            P("pipe", "tensor"),
            P("pipe", "dp", "tensor", None, None),
            P("pipe", "dp", "tensor"),
            P("pipe", "dp", "tensor"),
            P("pipe", "dp", "tensor"),
        ),
        out_specs=(
            P("pipe", "dp", "tensor", None, None),
            P("pipe", "dp", "tensor", None, None),
            P("pipe", "dp", "tensor", None, None),
        ),
        check_vma=False,
    )
```

profile of v0, /device:TPU:2, one launch (start us, length us, event | category | flops | bytes accessed | tf_op | source)
XLA Modules:
  0.0 350.0 jit_solution(13440303011730557698)
XLA Ops:
  7.2 2.4 copy.37
  9.7 0.7 copy.32
  10.4 15.2 %all-to-all-start = ((s32[1,16,1]{2,0,1:T(1,128)}), s32[1,16,1]{2,0,1:T(1,128)S(1)}, u32[]{:S(2)}, u32[]{:S(2)}) async-start(s32[1,16,1]{2,0,1:T(1,128)} %copy.32), calls=%async_computation | async-start | bytes 16384 | tf_op jit(solution)/shard_map/all_to_all | solution.py:52
  25.6 1.7 copy.33
  27.3 2.1 copy.34
  29.4 0.9 gather_fusion
  30.3 1.8 fusion.8
  32.1 5.8 %all-to-all-done = s32[1,16,1]{2,0,1:T(1,128)S(1)} async-done(((s32[1,16,1]{2,0,1:T(1,128)}), s32[1,16,1]{2,0,1:T(1,128)S(1)}, u32[]{:S(2)}, u32[]{:S(2)}) %all-to-all-start) | async-done | bytes 96 | tf_op jit(solution)/shard_map/all_to_all | solution.py:52
  38.0 6.3 %all-to-all-start.1 = ((bf16[384,16,128]{2,0,1:T(8,128)(2,1)}), bf16[384,16,128]{2,0,1:T(8,128)(2,1)S(1)}, u32[]{:S(2)}, u32[]{:S(2)}) async-start(bf16[384,16,128]{2,0,1:T(8,128)(2,1)} %fusion.8), calls=%async_computation.1 | async-start | bytes 3145728 | tf_op jit(solution)/shard_map/all_to_all | solution.py:51
  44.4 186.3 %all-gather.3.cloned.1.call-done = bf16[1,384,16384]{1,2,0:T(8,128)(2,1)} async-done(((bf16[1,384,1024]{1,2,0:T(8,128)(2,1)}), bf16[1,384,16384]{1,2,0:T(8,128)(2,1)}) %all-gather.3.cloned.1.call-update) | async-done | bytes 12582928 | tf_op jit(solution)/shard_map/all_gather | solution.py:35
  230.7 15.8 %copy.38 = bf16[384,128,128]{2,0,1:T(8,128)(2,1)} copy(bf16[384,128,128]{0,2,1:T(8,128)(2,1)} %bitcast.64) | data formatting | bytes 25165824 | tf_op jit(solution)/shard_map/reshape | solution.py:37
  246.5 6.6 %gather_fusion.2 = bf16[16,384,128]{2,1,0:T(8,128)(2,1)} fusion(bf16[384,128,128]{2,0,1:T(8,128)(2,1)} %copy.38, s32[1024]{0:T(1024)S(1)} %pad_clamp_fusion), kind=kCustom, calls=%fused_computation.2 | custom fusion | bytes 3145792 | tf_op jit(solution)/shard_map/jit(_take)/gather | solution.py:36
  253.1 4.1 %broadcast_select_fusion.3 = (f32[16,128,128]{2,1,0:T(8,128)}, f32[1,1,16,128,128]{4,3,2,1,0:T(8,128)}) fusion(pred[16]{0:T(512)(128)(4,1)S(1)} %compare_bitcast_fusion, f32[1,1,16,128,128]{4,3,2,1,0:T(8,128)S(1)} %copy-done.3, bf16[16,384,128]{2,1,0:T(8,128)(2,1)} %copy-done.1, pred[16]{0:T(512)(128)(4,1)S(1)} %compare_and_fusion.1, ...), kind=kOutput, calls=%fused_computation.21 | convolution fusion | flops 203948032 | bytes 6291504 | tf_op jit(solution)/shard_map/tkc,tkf->kcf/dot_general | solution.py:39
  257.2 0.4 reduce
  257.6 0.9 fusion.24
  258.6 1.9 collective-permute-start.1
  260.5 2.4 collective-permute-start.2
  262.9 1.9 collective-permute-start
  264.9 1.4 collective-permute-done
  266.2 0.6 iota_compare_fusion.1
  266.9 0.2 copy.36
  267.1 0.7 gather_fusion.1
  267.8 0.8 bitcast_select_fusion
  268.6 74.6 %reduce-scatter.4.cloned.1.call-done = f32[1,128,128]{2,1,0:T(8,128)} async-done(((f32[16,128,128]{2,1,0:T(8,128)}), f32[1,128,128]{2,1,0:T(8,128)}) %reduce-scatter.4.cloned.1.call-update) | async-done | bytes 65552
  (32 shorter events, 0.2 us)
Async XLA Ops:
  7.2 23.1 %copy-start = (bf16[1,16,128,128]{3,2,1,0:T(8,128)(2,1)S(1)}, bf16[1,16,128,128]{3,2,1,0:T(8,128)(2,1)}, u32[]{:S(2)}) copy-start(bf16[1,16,128,128]{3,2,1,0:T(8,128)(2,1)} %param.11) | copy-start | bytes 1572868
  7.2 2.5 copy-start.5
  7.2 18.4 %copy-start.2 = (bf16[1,384,1664]{2,1,0:T(8,128)(2,1)S(1)}, bf16[1,384,1664]{2,1,0:T(8,128)(2,1)}, u32[]{:S(2)}) copy-start(bf16[1,384,1664]{2,1,0:T(8,128)(2,1)} %param.10) | copy-start | bytes 3833860
  7.2 223.5 %all-gather.3.cloned.1.call-start = ((), (), s32[]{:S(2)}) async-start(), calls=%async_computation.3 | async-start | bytes 13369344 | tf_op jit(solution)/shard_map/all_gather | solution.py:35
  10.4 27.6 %all-to-all-start = ((s32[1,16,1]{2,0,1:T(1,128)}), s32[1,16,1]{2,0,1:T(1,128)S(1)}, u32[]{:S(2)}, u32[]{:S(2)}) async-start(s32[1,16,1]{2,0,1:T(1,128)} %copy.32), calls=%async_computation | async-start | bytes 16384 | tf_op jit(solution)/shard_map/all_to_all | solution.py:52
  27.3 2.1 copy-start.4
  30.3 1.9 copy-start.1
  32.1 12.3 %copy-start.6 = (s32[1,1,16]{2,1,0:T(1,128)S(1)}, s32[1,1,16]{2,1,0:T(1,128)}, u32[]{:S(2)}) copy-start(s32[1,1,16]{2,1,0:T(1,128)} %param.15) | copy-start | bytes 196
  38.0 219.7 %all-to-all-start.1 = ((bf16[384,16,128]{2,0,1:T(8,128)(2,1)}), bf16[384,16,128]{2,0,1:T(8,128)(2,1)S(1)}, u32[]{:S(2)}, u32[]{:S(2)}) async-start(bf16[384,16,128]{2,0,1:T(8,128)(2,1)} %fusion.8), calls=%async_computation.1 | async-start | bytes 3145728 | tf_op jit(solution)/shard_map/all_to_all | solution.py:51
  44.3 298.9 %reduce-scatter.4.cloned.1.call-start = ((), (), s32[]{:S(2)}) async-start(), calls=%async_computation.4 | async-start | bytes 1114112
  246.5 6.6 %copy-start.3 = (f32[1,1,16,128,128]{4,3,2,1,0:T(8,128)S(1)}, f32[1,1,16,128,128]{4,3,2,1,0:T(8,128)}, u32[]{:S(2)}) copy-start(f32[1,1,16,128,128]{4,3,2,1,0:T(8,128)} %param.14) | copy-start | bytes 3145732
  257.2 3.3 copy-start.7
  258.6 8.3 %collective-permute-start.1 = (bf16[384,8,128]{2,1,0:T(8,128)(2,1)S(1)}, bf16[384,8,128]{2,1,0:T(8,128)(2,1)S(1)}, u32[]{:S(2)}, u32[]{:S(2)}) collective-permute-start(bf16[384,8,128]{2,1,0:T(8,128)(2,1)S(1)} %fusion.24), channel_id=1, source_target_pairs={{0,256},{256,0},{1,257},{257,1},{2,258},{258,2},{3,259},{259,3},{4... | collective-permute-start | bytes 2359304 | tf_op jit(solution)/shard_map/ppermute | solution.py:9
  260.5 6.3 %collective-permute-start.2 = (s32[12]{0:T(128)S(1)}, s32[12]{0:T(128)S(1)}, u32[]{:S(2)}, u32[]{:S(2)}) collective-permute-start(s32[12]{0:T(128)S(1)} %bitcast.68), channel_id=1, source_target_pairs={{0,256},{256,0},{1,257},{257,1},{2,258},{258,2},{3,259},{259,3},{4... | collective-permute-start | bytes 152 | tf_op jit(solution)/shard_map/ppermute | solution.py:9
  262.9 3.3 collective-permute-start
Sparse Core Ops, SparseCore 0:
  10.7 219.9 all-gather.2
  257.4 85.7 reduce-scatter.3
where the time goes:
time: 351 us; the launch traced here: 350 us
  waiting for transfers between devices  268 us (76%)
  local copies, waits for them, and re-layouts  31 us (9%)
  starting transfers between devices  27.9 us (8%)
  between operations  14.3 us (4%)
  matrix products  6.86 us (2%)
    all_gather x1, waiting for transfers between devices, local(): gathered = lax.all_gather(inputs, 'tensor', axis=1, tiled=True)  186 us
    unnamed x3, waiting for transfers between devices  74.6 us
    reshape x1, local copies, waits for them, and re-layouts, local(): gathered.reshape(tok_count, local_blocks * tensor_count, tile_size)  15.8 us
    all_to_all x1, starting transfers between devices, local(): lax.all_to_all(local_rows[None, :], 'tensor', split_axis=1, concat_axis=1...  15.2 us
  transfers between devices with their start and end apart: 7, of which 4 were waited for; matrix products, arithmetic and copies ran while one was open for 11% of the time, Pallas kernels for 0%

commit v1 on v0

--- a/solution.py
+++ b/solution.py
@@ -32,7 +32,14 @@
     local_rows = row_ids % local_blocks
     grad_blocks = grads_out.reshape(tok_count, grads_out.shape[1] // tile_size, tile_size)
     grad_sel = jnp.take(grad_blocks, col_ids, axis=1)
-    gathered = lax.all_gather(inputs, "tensor", axis=1, tiled=True)
+    ring = [inputs]
+    for hop in range(15):
+        ring.append(lax.ppermute(ring[-1], "tensor", [(dev, (dev + 1) % 16) for dev in range(16)]))
+    gathered = jnp.roll(
+        jnp.concatenate(ring[::-1], axis=1),
+        (lax.axis_index("tensor") + 1) * ring[0].shape[1],
+        axis=1,
+    )
     input_sel = jnp.take(
         gathered.reshape(tok_count, local_blocks * tensor_count, tile_size), row_ids, axis=1
     )

time: 351 us -> 525 us (1.50)
  local copies, waits for them, and re-layouts: 31 us -> 117 us
  waiting for transfers between devices: 268 us -> 319 us
  starting transfers between devices: 27.9 us -> 57.1 us
    ppermute x0 -> x15, waiting for transfers between devices: none -> 240 us  [local(): lax.ppermute(ring[-1], 'tensor', [(dev, (dev + 1) % 16) for dev in range(...]
    all_gather x1 -> x0, waiting for transfers between devices: 186 us -> none  [local(): gathered = lax.all_gather(inputs, 'tensor', axis=1, tiled=True)]
    unnamed x18 -> x65, local copies, waits for them, and re-layouts: 4.14 us -> 77 us
    ppermute x0 -> x15, starting transfers between devices: none -> 30.5 us  [local(): lax.ppermute(ring[-1], 'tensor', [(dev, (dev + 1) % 16) for dev in range(...]
    dynamic_slice x0 -> x1, local copies, waits for them, and re-layouts: none -> 10.6 us  [local(): jnp.roll(jnp.concatenate(ring[::-1], axis=1), (lax.axis_index('tensor') +...]
    all_to_all x1, waiting for transfers between devices: 5.83 us -> 0.01 us  [local(): lax.all_to_all(local_rows[None, :], 'tensor', split_axis=1, concat_axis=1...]
    unnamed x3 -> x2, waiting for transfers between devices: 74.6 us -> 78.1 us
  transfers between devices with their start and end apart: 7 -> 21, of which waited for: 4 -> 17; matrix products, arithmetic and copies ran while one was open for 11% -> 23% of each run, Pallas kernels for 0% -> 0%
where the time goes in v1:
time: 525 us; the launch traced here: 523 us
  waiting for transfers between devices  319 us (61%)
  local copies, waits for them, and re-layouts  117 us (22%)
  starting transfers between devices  57.1 us (11%)
  between operations  14.3 us (3%)
  matrix products  8.48 us (2%)
  other arithmetic  5.91 us (1%)
    ppermute x15, waiting for transfers between devices, local(): lax.ppermute(ring[-1], 'tensor', [(dev, (dev + 1) % 16) for dev in range(...  240 us
    unnamed x2, waiting for transfers between devices  78.1 us
    unnamed x65, local copies, waits for them, and re-layouts  77 us
    ppermute x15, starting transfers between devices, local(): lax.ppermute(ring[-1], 'tensor', [(dev, (dev + 1) % 16) for dev in range(...  30.5 us
    reshape x1, local copies, waits for them, and re-layouts, local(): gathered.reshape(tok_count, local_blocks * tensor_count, tile_size)  16.7 us
    dynamic_slice x1, local copies, waits for them, and re-layouts, local(): jnp.roll(jnp.concatenate(ring[::-1], axis=1), (lax.axis_index('tensor') +...  10.6 us
  transfers between devices with their start and end apart: 21, of which 17 were waited for; matrix products, arithmetic and copies ran while one was open for 23% of the time, Pallas kernels for 0%

profile of v1, /device:TPU:2, one launch (start us, length us, event | category | flops | bytes accessed | tf_op | source)
XLA Modules:
  0.0 522.6 jit_solution(13769994064153454400)
XLA Ops:
  8.7 3.8 collective-permute-start.3
  12.6 25.1 %collective-permute-done.3 = bf16[384,1024]{0,1:T(8,128)(2,1)S(1)} collective-permute-done((bf16[384,1024]{0,1:T(8,128)(2,1)S(1)}, bf16[384,1024]{0,1:T(8,128)(2,1)S(1)}, u32[]{:S(2)}, u32[]{:S(2)}) %collective-permute-start.3) | collective-permute-done | bytes 786464 | tf_op jit(solution)/shard_map/ppermute | solution.py:37
  40.5 19.9 %collective-permute-done.4 = bf16[384,1024]{0,1:T(8,128)(2,1)S(1)} collective-permute-done((bf16[384,1024]{0,1:T(8,128)(2,1)S(1)}, bf16[384,1024]{0,1:T(8,128)(2,1)S(1)}, u32[]{:S(2)}, u32[]{:S(2)}) %collective-permute-start.4) | collective-permute-done | bytes 786464 | tf_op jit(solution)/shard_map/ppermute | solution.py:37
  62.3 19.0 %collective-permute-done.5 = bf16[384,1024]{0,1:T(8,128)(2,1)S(1)} collective-permute-done((bf16[384,1024]{0,1:T(8,128)(2,1)S(1)}, bf16[384,1024]{0,1:T(8,128)(2,1)S(1)}, u32[]{:S(2)}, u32[]{:S(2)}) %collective-permute-start.5) | collective-permute-done | bytes 786464 | tf_op jit(solution)/shard_map/ppermute | solution.py:37
  84.1 18.1 %collective-permute-done.6 = bf16[384,1024]{0,1:T(8,128)(2,1)S(1)} collective-permute-done((bf16[384,1024]{0,1:T(8,128)(2,1)S(1)}, bf16[384,1024]{0,1:T(8,128)(2,1)S(1)}, u32[]{:S(2)}, u32[]{:S(2)}) %collective-permute-start.6) | collective-permute-done | bytes 786464 | tf_op jit(solution)/shard_map/ppermute | solution.py:37
  105.0 17.1 %collective-permute-done.7 = bf16[384,1024]{0,1:T(8,128)(2,1)S(1)} collective-permute-done((bf16[384,1024]{0,1:T(8,128)(2,1)S(1)}, bf16[384,1024]{0,1:T(8,128)(2,1)S(1)}, u32[]{:S(2)}, u32[]{:S(2)}) %collective-permute-start.7) | collective-permute-done | bytes 786464 | tf_op jit(solution)/shard_map/ppermute | solution.py:37
  124.9 16.2 %collective-permute-done.8 = bf16[384,1024]{0,1:T(8,128)(2,1)S(1)} collective-permute-done((bf16[384,1024]{0,1:T(8,128)(2,1)S(1)}, bf16[384,1024]{0,1:T(8,128)(2,1)S(1)}, u32[]{:S(2)}, u32[]{:S(2)}) %collective-permute-start.8) | collective-permute-done | bytes 786464 | tf_op jit(solution)/shard_map/ppermute | solution.py:37
  144.0 15.3 %collective-permute-done.9 = bf16[384,1024]{0,1:T(8,128)(2,1)S(1)} collective-permute-done((bf16[384,1024]{0,1:T(8,128)(2,1)S(1)}, bf16[384,1024]{0,1:T(8,128)(2,1)S(1)}, u32[]{:S(2)}, u32[]{:S(2)}) %collective-permute-start.9) | collective-permute-done | bytes 786464 | tf_op jit(solution)/shard_map/ppermute | solution.py:37
  162.1 14.9 %collective-permute-done.10 = bf16[384,1024]{0,1:T(8,128)(2,1)S(1)} collective-permute-done((bf16[384,1024]{0,1:T(8,128)(2,1)S(1)}, bf16[384,1024]{0,1:T(8,128)(2,1)S(1)}, u32[]{:S(2)}, u32[]{:S(2)}) %collective-permute-start.10) | collective-permute-done | bytes 786464 | tf_op jit(solution)/shard_map/ppermute | solution.py:37
  179.8 14.9 %collective-permute-done.11 = bf16[384,1024]{0,1:T(8,128)(2,1)S(1)} collective-permute-done((bf16[384,1024]{0,1:T(8,128)(2,1)S(1)}, bf16[384,1024]{0,1:T(8,128)(2,1)S(1)}, u32[]{:S(2)}, u32[]{:S(2)}) %collective-permute-start.11) | collective-permute-done | bytes 786464 | tf_op jit(solution)/shard_map/ppermute | solution.py:37
  197.5 15.6 %collective-permute-done.12 = bf16[384,1024]{0,1:T(8,128)(2,1)S(1)} collective-permute-done((bf16[384,1024]{0,1:T(8,128)(2,1)S(1)}, bf16[384,1024]{0,1:T(8,128)(2,1)S(1)}, u32[]{:S(2)}, u32[]{:S(2)}) %collective-permute-start.12) | collective-permute-done | bytes 786464 | tf_op jit(solution)/shard_map/ppermute | solution.py:37
  216.0 16.7 %collective-permute-done.13 = bf16[384,1024]{0,1:T(8,128)(2,1)S(1)} collective-permute-done((bf16[384,1024]{0,1:T(8,128)(2,1)S(1)}, bf16[384,1024]{0,1:T(8,128)(2,1)S(1)}, u32[]{:S(2)}, u32[]{:S(2)}) %collective-permute-start.13) | collective-permute-done | bytes 786464 | tf_op jit(solution)/shard_map/ppermute | solution.py:37
  235.5 17.8 %collective-permute-done.14 = bf16[384,1024]{0,1:T(8,128)(2,1)S(1)} collective-permute-done((bf16[384,1024]{0,1:T(8,128)(2,1)S(1)}, bf16[384,1024]{0,1:T(8,128)(2,1)S(1)}, u32[]{:S(2)}, u32[]{:S(2)}) %collective-permute-start.14) | collective-permute-done | bytes 786464 | tf_op jit(solution)/shard_map/ppermute | solution.py:37
  256.1 19.8 %collective-permute-done.15 = bf16[384,1024]{0,1:T(8,128)(2,1)S(1)} collective-permute-done((bf16[384,1024]{0,1:T(8,128)(2,1)S(1)}, bf16[384,1024]{0,1:T(8,128)(2,1)S(1)}, u32[]{:S(2)}, u32[]{:S(2)}) %collective-permute-start.15) | collective-permute-done | bytes 786464 | tf_op jit(solution)/shard_map/ppermute | solution.py:37
  279.1 10.0 %all-to-all-start = ((s32[1,16,1]{2,0,1:T(1,128)}), s32[1,16,1]{2,0,1:T(1,128)S(1)}, u32[]{:S(2)}, u32[]{:S(2)}) async-start(s32[1,16,1]{2,0,1:T(1,128)} %copy.32), calls=%async_computation | async-start | bytes 16384 | tf_op jit(solution)/shard_map/all_to_all | solution.py:59
  291.1 7.4 %collective-permute-done.16 = bf16[384,1024]{0,1:T(8,128)(2,1)} collective-permute-done((bf16[384,1024]{0,1:T(8,128)(2,1)S(1)}, bf16[384,1024]{0,1:T(8,128)(2,1)}, u32[]{:S(2)}, u32[]{:S(2)}) %collective-permute-start.16) | collective-permute-done | bytes 786464 | tf_op jit(solution)/shard_map/ppermute | solution.py:37
  300.4 2.5 copy.33
  308.4 3.2 fusion.8
  342.3 10.3 %all-to-all-start.1 = ((bf16[384,16,128]{2,0,1:T(8,128)(2,1)}), bf16[384,16,128]{2,0,1:T(8,128)(2,1)S(1)}, u32[]{:S(2)}, u32[]{:S(2)}) async-start(bf16[384,16,128]{2,0,1:T(8,128)(2,1)} %fusion.8), calls=%async_computation.1 | async-start | bytes 3145728 | tf_op jit(solution)/shard_map/all_to_all | solution.py:58
  388.3 10.6 %constant_dynamic-slice_fusion = bf16[384,16384]{0,1:T(8,128)(2,1)} fusion(bf16[384,32768]{0,1:T(8,128)(2,1)} %constant_dynamic-update-slice_fusion, s32[]{:T(128)S(6)} %select_n.102), kind=kLoop, calls=%fused_computation.87 | loop fusion | bytes 25165828 | tf_op jit(solution)/shard_map/jit(_roll_dynamic)/dynamic_slice | solution.py:38
  398.9 16.7 %copy.38 = bf16[384,128,128]{2,0,1:T(8,128)(2,1)} copy(bf16[384,128,128]{0,2,1:T(8,128)(2,1)} %bitcast.67) | data formatting | bytes 25165824 | tf_op jit(solution)/shard_map/reshape | solution.py:44
  415.6 6.5 %gather_fusion.2 = bf16[16,384,128]{2,1,0:T(8,128)(2,1)} fusion(bf16[384,128,128]{2,0,1:T(8,128)(2,1)} %copy.38, s32[1024]{0:T(1024)S(1)} %pad_clamp_fusion), kind=kCustom, calls=%fused_computation.2 | custom fusion | bytes 3145792 | tf_op jit(solution)/shard_map/jit(_take)/gather | solution.py:43
  422.0 4.4 broadcast_select_fusion.3
  437.7 78.1 %reduce-scatter.4.cloned.1.call-done = f32[1,128,128]{2,1,0:T(8,128)} async-done(((f32[16,128,128]{2,1,0:T(8,128)}), f32[1,128,128]{2,1,0:T(8,128)}) %reduce-scatter.4.cloned.1.call-update) | async-done | bytes 65552
  (108 shorter events, 124.5 us)
Async XLA Ops:
  7.2 301.2 %copy-start = (bf16[1,16,128,128]{3,2,1,0:T(8,128)(2,1)S(1)}, bf16[1,16,128,128]{3,2,1,0:T(8,128)(2,1)}, u32[]{:S(2)}) copy-start(bf16[1,16,128,128]{3,2,1,0:T(8,128)(2,1)} %param.11) | copy-start | bytes 1572868
  8.7 28.9 %collective-permute-start.3 = (bf16[384,1024]{0,1:T(8,128)(2,1)S(1)}, bf16[384,1024]{0,1:T(8,128)(2,1)S(1)}, u32[]{:S(2)}, u32[]{:S(2)}) collective-permute-start(bf16[384,1024]{0,1:T(8,128)(2,1)S(1)} %bitcast.68), channel_id=1, source_target_pairs={{0,1},{1,2},{2,3},{3,4},{4,5},{5,6},{6,7},{7,8},{8,9},{9,10},{10,1... | collective-permute-start | bytes 2359304 | tf_op jit(solution)/shard_map/ppermute | solution.py:37
  38.6 21.8 %collective-permute-start.4 = (bf16[384,1024]{0,1:T(8,128)(2,1)S(1)}, bf16[384,1024]{0,1:T(8,128)(2,1)S(1)}, u32[]{:S(2)}, u32[]{:S(2)}) collective-permute-start(bf16[384,1024]{0,1:T(8,128)(2,1)S(1)} %collective-permute-done.3), channel_id=1, source_target_pairs={{0,1},{1,2},{2,3},{3,4},{4,5},{5,6},{6,7},{7,8},{8,9},{9,10},{10,1... | collective-permute-start | bytes 2359304 | tf_op jit(solution)/shard_map/ppermute | solution.py:37
  60.4 281.9 %copy-start.3 = (bf16[384,1024]{0,1:T(8,128)(2,1)}, bf16[384,1024]{0,1:T(8,128)(2,1)S(1)}, u32[]{:S(2)}) copy-start(bf16[384,1024]{0,1:T(8,128)(2,1)S(1)} %collective-permute-done.4) | copy-start | bytes 2359300
  60.4 20.9 %collective-permute-start.5 = (bf16[384,1024]{0,1:T(8,128)(2,1)S(1)}, bf16[384,1024]{0,1:T(8,128)(2,1)S(1)}, u32[]{:S(2)}, u32[]{:S(2)}) collective-permute-start(bf16[384,1024]{0,1:T(8,128)(2,1)S(1)} %collective-permute-done.4), channel_id=1, source_target_pairs={{0,1},{1,2},{2,3},{3,4},{4,5},{5,6},{6,7},{7,8},{8,9},{9,10},{10,1... | collective-permute-start | bytes 2359304 | tf_op jit(solution)/shard_map/ppermute | solution.py:37
  82.2 20.0 %collective-permute-start.6 = (bf16[384,1024]{0,1:T(8,128)(2,1)S(1)}, bf16[384,1024]{0,1:T(8,128)(2,1)S(1)}, u32[]{:S(2)}, u32[]{:S(2)}) collective-permute-start(bf16[384,1024]{0,1:T(8,128)(2,1)S(1)} %collective-permute-done.5), channel_id=1, source_target_pairs={{0,1},{1,2},{2,3},{3,4},{4,5},{5,6},{6,7},{7,8},{8,9},{9,10},{10,1... | collective-permute-start | bytes 2359304 | tf_op jit(solution)/shard_map/ppermute | solution.py:37
  103.1 19.1 %collective-permute-start.7 = (bf16[384,1024]{0,1:T(8,128)(2,1)S(1)}, bf16[384,1024]{0,1:T(8,128)(2,1)S(1)}, u32[]{:S(2)}, u32[]{:S(2)}) collective-permute-start(bf16[384,1024]{0,1:T(8,128)(2,1)S(1)} %collective-permute-done.6), channel_id=1, source_target_pairs={{0,1},{1,2},{2,3},{3,4},{4,5},{5,6},{6,7},{7,8},{8,9},{9,10},{10,1... | collective-permute-start | bytes 2359304 | tf_op jit(solution)/shard_map/ppermute | solution.py:37
  123.0 18.1 %collective-permute-start.8 = (bf16[384,1024]{0,1:T(8,128)(2,1)S(1)}, bf16[384,1024]{0,1:T(8,128)(2,1)S(1)}, u32[]{:S(2)}, u32[]{:S(2)}) collective-permute-start(bf16[384,1024]{0,1:T(8,128)(2,1)S(1)} %collective-permute-done.7), channel_id=1, source_target_pairs={{0,1},{1,2},{2,3},{3,4},{4,5},{5,6},{6,7},{7,8},{8,9},{9,10},{10,1... | collective-permute-start | bytes 2359304 | tf_op jit(solution)/shard_map/ppermute | solution.py:37
  142.1 17.2 %collective-permute-start.9 = (bf16[384,1024]{0,1:T(8,128)(2,1)S(1)}, bf16[384,1024]{0,1:T(8,128)(2,1)S(1)}, u32[]{:S(2)}, u32[]{:S(2)}) collective-permute-start(bf16[384,1024]{0,1:T(8,128)(2,1)S(1)} %collective-permute-done.8), channel_id=1, source_target_pairs={{0,1},{1,2},{2,3},{3,4},{4,5},{5,6},{6,7},{7,8},{8,9},{9,10},{10,1... | collective-permute-start | bytes 2359304 | tf_op jit(solution)/shard_map/ppermute | solution.py:37
  160.2 16.8 %collective-permute-start.10 = (bf16[384,1024]{0,1:T(8,128)(2,1)S(1)}, bf16[384,1024]{0,1:T(8,128)(2,1)S(1)}, u32[]{:S(2)}, u32[]{:S(2)}) collective-permute-start(bf16[384,1024]{0,1:T(8,128)(2,1)S(1)} %collective-permute-done.9), channel_id=1, source_target_pairs={{0,1},{1,2},{2,3},{3,4},{4,5},{5,6},{6,7},{7,8},{8,9},{9,10},{10,1... | collective-permute-start | bytes 2359304 | tf_op jit(solution)/shard_map/ppermute | solution.py:37
  177.9 16.8 %collective-permute-start.11 = (bf16[384,1024]{0,1:T(8,128)(2,1)S(1)}, bf16[384,1024]{0,1:T(8,128)(2,1)S(1)}, u32[]{:S(2)}, u32[]{:S(2)}) collective-permute-start(bf16[384,1024]{0,1:T(8,128)(2,1)S(1)} %collective-permute-done.10), channel_id=1, source_target_pairs={{0,1},{1,2},{2,3},{3,4},{4,5},{5,6},{6,7},{7,8},{8,9},{9,10},{10,1... | collective-permute-start | bytes 2359304 | tf_op jit(solution)/shard_map/ppermute | solution.py:37
  195.6 17.5 %collective-permute-start.12 = (bf16[384,1024]{0,1:T(8,128)(2,1)S(1)}, bf16[384,1024]{0,1:T(8,128)(2,1)S(1)}, u32[]{:S(2)}, u32[]{:S(2)}) collective-permute-start(bf16[384,1024]{0,1:T(8,128)(2,1)S(1)} %collective-permute-done.11), channel_id=1, source_target_pairs={{0,1},{1,2},{2,3},{3,4},{4,5},{5,6},{6,7},{7,8},{8,9},{9,10},{10,1... | collective-permute-start | bytes 2359304 | tf_op jit(solution)/shard_map/ppermute | solution.py:37
  214.0 18.6 %collective-permute-start.13 = (bf16[384,1024]{0,1:T(8,128)(2,1)S(1)}, bf16[384,1024]{0,1:T(8,128)(2,1)S(1)}, u32[]{:S(2)}, u32[]{:S(2)}) collective-permute-start(bf16[384,1024]{0,1:T(8,128)(2,1)S(1)} %collective-permute-done.12), channel_id=1, source_target_pairs={{0,1},{1,2},{2,3},{3,4},{4,5},{5,6},{6,7},{7,8},{8,9},{9,10},{10,1... | collective-permute-start | bytes 2359304 | tf_op jit(solution)/shard_map/ppermute | solution.py:37
  233.5 19.7 %collective-permute-start.14 = (bf16[384,1024]{0,1:T(8,128)(2,1)S(1)}, bf16[384,1024]{0,1:T(8,128)(2,1)S(1)}, u32[]{:S(2)}, u32[]{:S(2)}) collective-permute-start(bf16[384,1024]{0,1:T(8,128)(2,1)S(1)} %collective-permute-done.13), channel_id=1, source_target_pairs={{0,1},{1,2},{2,3},{3,4},{4,5},{5,6},{6,7},{7,8},{8,9},{9,10},{10,1... | collective-permute-start | bytes 2359304 | tf_op jit(solution)/shard_map/ppermute | solution.py:37
  254.1 21.7 %collective-permute-start.15 = (bf16[384,1024]{0,1:T(8,128)(2,1)S(1)}, bf16[384,1024]{0,1:T(8,128)(2,1)S(1)}, u32[]{:S(2)}, u32[]{:S(2)}) collective-permute-start(bf16[384,1024]{0,1:T(8,128)(2,1)S(1)} %collective-permute-done.14), channel_id=1, source_target_pairs={{0,1},{1,2},{2,3},{3,4},{4,5},{5,6},{6,7},{7,8},{8,9},{9,10},{10,1... | collective-permute-start | bytes 2359304 | tf_op jit(solution)/shard_map/ppermute | solution.py:37
  275.9 22.6 %collective-permute-start.16 = (bf16[384,1024]{0,1:T(8,128)(2,1)S(1)}, bf16[384,1024]{0,1:T(8,128)(2,1)}, u32[]{:S(2)}, u32[]{:S(2)}) collective-permute-start(bf16[384,1024]{0,1:T(8,128)(2,1)S(1)} %collective-permute-done.15), channel_id=1, source_target_pairs={{0,1},{1,2},{2,3},{3,4},{4,5},{5,6},{6,7},{7,8},{8,9},{9,10},{10,1... | collective-permute-start | bytes 2359304 | tf_op jit(solution)/shard_map/ppermute | solution.py:37
  279.1 63.2 %all-to-all-start = ((s32[1,16,1]{2,0,1:T(1,128)}), s32[1,16,1]{2,0,1:T(1,128)S(1)}, u32[]{:S(2)}, u32[]{:S(2)}) async-start(s32[1,16,1]{2,0,1:T(1,128)} %copy.32), calls=%async_computation | async-start | bytes 16384 | tf_op jit(solution)/shard_map/all_to_all | solution.py:59
  298.5 15.4 %collective-permute-start.17 = (bf16[384,1024]{0,1:T(8,128)(2,1)}, bf16[384,1024]{0,1:T(8,128)(2,1)}, u32[]{:S(2)}, u32[]{:S(2)}) collective-permute-start(bf16[384,1024]{0,1:T(8,128)(2,1)} %collective-permute-done.16), channel_id=1, source_target_pairs={{0,1},{1,2},{2,3},{3,4},{4,5},{5,6},{6,7},{7,8},{8,9},{9,10},{10,1... | collective-permute-start | bytes 2359304 | tf_op jit(solution)/shard_map/ppermute | solution.py:37
  342.3 84.5 %all-to-all-start.1 = ((bf16[384,16,128]{2,0,1:T(8,128)(2,1)}), bf16[384,16,128]{2,0,1:T(8,128)(2,1)S(1)}, u32[]{:S(2)}, u32[]{:S(2)}) async-start(bf16[384,16,128]{2,0,1:T(8,128)(2,1)} %fusion.8), calls=%async_computation.1 | async-start | bytes 3145728 | tf_op jit(solution)/shard_map/all_to_all | solution.py:58
  352.6 163.2 %reduce-scatter.4.cloned.1.call-start = ((), (), s32[]{:S(2)}) async-start(), calls=%async_computation.3 | async-start | bytes 1114112
  388.3 127.5 %copy-start.1 = (bf16[1,16,128,128]{3,2,1,0:T(8,128)(2,1)S(1)}, bf16[1,16,128,128]{3,2,1,0:T(8,128)(2,1)}, u32[]{:S(2)}) copy-start(bf16[1,16,128,128]{3,2,1,0:T(8,128)(2,1)} %param.11) | copy-start | bytes 1572868
  427.8 8.2 %collective-permute-start.1 = (bf16[384,8,128]{2,1,0:T(8,128)(2,1)S(1)}, bf16[384,8,128]{2,1,0:T(8,128)(2,1)S(1)}, u32[]{:S(2)}, u32[]{:S(2)}) collective-permute-start(bf16[384,8,128]{2,1,0:T(8,128)(2,1)S(1)} %fusion.24), channel_id=1, source_target_pairs={{0,256},{256,0},{1,257},{257,1},{2,258},{258,2},{3,259},{259,3},{4... | collective-permute-start | bytes 2359304 | tf_op jit(solution)/shard_map/ppermute | solution.py:9
  429.7 6.2 %collective-permute-start.2 = (s32[12]{0:T(128)S(1)}, s32[12]{0:T(128)S(1)}, u32[]{:S(2)}, u32[]{:S(2)}) collective-permute-start(s32[12]{0:T(128)S(1)} %bitcast.72), channel_id=1, source_target_pairs={{0,256},{256,0},{1,257},{257,1},{2,258},{258,2},{3,259},{259,3},{4... | collective-permute-start | bytes 152 | tf_op jit(solution)/shard_map/ppermute | solution.py:9
  432.1 3.1 collective-permute-start
  (13 other events, 67.8 us)
Sparse Core Ops, SparseCore 0:
  426.5 89.1 reduce-scatter.3
